TPU v7x, 128 devices: a whole 4x4x4 slice. The times are simulated.
128 devices in a mesh: outer: 2 (over y_hi), inner: 64 (over y_lo, z, x, core).
Axes of the slice: x: 4, y: 4 (y_hi: 2, y_lo: 2; y = y_hi * 2 + y_lo), z: 4, core: 2. Of those that a mesh axis runs over, the one named last changes fastest.
Arguments:
- queries: bfloat16 [40960, 2048], P(('outer', 'inner')), may hold values from -300 to 300
- keys: bfloat16 [40960, 128], P(('outer', 'inner')), may hold values from -6 to 6
- values: bfloat16 [40960, 128], P(('outer', 'inner')), may hold values from -6 to 6
- doc_lengths: int32 [64], replicated, may hold values from 1 to 4800, 40960 in all
Outputs:
- attended: bfloat16 [40960, 2048], P(('outer', 'inner'))
Inputs may be any that keep to these rules, and one draw needn't show every extreme that they name: `doc_lengths`: the lengths sum to 40960; the longest document has exactly 4800 tokens.
All inputs are finite; a program needn't handle non-finite values.
Results may differ from a plain program's by a relative error of at most 0.0036.
Values may be sent and summed in bfloat16 or wider, within the bound.
No kernel may reach another device: no remote copies, remote signals or barrier semaphores. Data moves between devices by JAX's collectives and lax.ppermute only.
A program may use at most 64 MiB of HBM per device.

v0:
```python
import functools

import jax
import jax.numpy as jnp
from jax import lax
from jax.experimental import pallas as pl
from jax.experimental.pallas import tpu as pltpu
from jax.sharding import PartitionSpec as P

AXES = ("outer", "inner")
ROW = 8
TOK = 320
HD = 128
HEADS = 16
GROUP = 8
GROUPS = HEADS // GROUP
M = GROUP * TOK
NDOCS = 64
DEVICES = 128
SCALE = 1.4426950408889634 / HD**0.5
NEVER = -1e30
NEW, OLD, THIRD = [pl.ds(i * 2 * TOK, 2 * TOK) for i in range(3)]
F32 = jnp.float32
BF16 = jnp.bfloat16
MIB = 2**20


def place():
    device = lax.axis_index("outer") * 64 + lax.axis_index("inner")
    return device, lax.rem(device, 2)


def columns(g, width=M):
    return pl.ds(g * width if isinstance(g, int) else pl.multiple_of(g * width, width), width)


def dot(a, b):
    return jnp.dot(a, b, preferred_element_type=F32)


def fold(p):
    return functools.reduce(lambda a, b: a + b, [p[i : i + 8] for i in range(0, p.shape[0], 8)])


def causal(begin):
    key = lax.broadcasted_iota(jnp.int32, (TOK, TOK), 0)
    row = lax.broadcasted_iota(jnp.int32, (TOK, TOK), 1)
    return jnp.where((key <= row) & (key >= begin), F32(0), F32(NEVER))


def pack_kernel(k_hbm, v_hbm, kv_ref, sems):
    copies = [
        pltpu.make_async_copy(half, kv_ref.at[pl.ds(i * TOK, TOK)], sems.at[i])
        for i, half in enumerate((k_hbm, v_hbm))
    ]
    for copy in copies:
        copy.start()
    for copy in copies:
        copy.wait()


def own_kernel(
    docs_hbm, q_hbm, kv_ref, qt_ref, acc_ref, tot_ref, begin_ref, first_ref,
    bias_ref, q_ref, docs, sems, docs_sem,
):
    read_docs = pltpu.make_async_copy(docs_hbm, docs, docs_sem)
    read_docs.start()

    def read(g):
        wide = columns(g, GROUP * HD)
        return pltpu.make_async_copy(q_hbm.at[:, wide], q_ref.at[:, wide], sems.at[g])

    for g in range(GROUPS):
        read(g).start()
    read_docs.wait()
    device, _ = place()
    token = lax.broadcasted_iota(jnp.int32, (1, TOK), 1)
    end = -device * TOK
    first = end
    begin = jnp.full((1, TOK), end, jnp.int32)
    for i in range(NDOCS):
        end = end + docs[i]
        begin = jnp.where(end <= token, end, begin)
        first = jnp.where(end <= 0, end, first)
    first_ref[0] = first
    begin_ref[...] = jnp.concatenate([begin] * GROUP, 1)
    bias_ref[...] = jnp.concatenate([causal(begin)] * GROUP, 1)
    qt_ref[HD:, :] = jnp.zeros((HD, HEADS * TOK), BF16)
    k = kv_ref[:TOK]
    vt = kv_ref[TOK:].T
    wide = 1

    for c in range(GROUPS // wide):
        for i in range(wide):
            read(c * wide + i).wait()
        heads = [q_ref[:, columns(c * wide * GROUP + i, HD)] for i in range(wide * GROUP)]
        qt = jnp.concatenate(heads, 0).T
        at = columns(c, wide * M)
        qt_ref[:HD, at] = qt
        s = dot(k, qt) + jnp.concatenate([bias_ref[...]] * wide, 1)
        m = jnp.max(s, 0, keepdims=True)
        p = jnp.exp2((s - m) * SCALE)
        tot_ref[:, at] = fold(p)
        acc_ref[:, at] = dot(vt, p.astype(BF16))
        begins = jnp.concatenate([begin_ref[...]] * wide, 1)
        shift = jnp.where(begins < 0, -m, F32(NEVER))
        line = lax.broadcasted_iota(jnp.int32, (16, wide * M), 0)
        extra = jnp.where(line == 3, F32(1), F32(0))
        for i in range(3):
            part = shift.astype(BF16).astype(F32)
            extra = jnp.where(line == i, part, extra)
            shift = shift - part
        qt_ref[HD : HD + 16, at] = extra.astype(BF16)


def fill(blocks, first, k_ref, vt_ref):
    for i, (block, position) in enumerate(blocks):
        rows = slice(i * TOK, (i + 1) * TOK)
        k_ref[rows, :HD] = block[:TOK]
        key = lax.broadcasted_iota(jnp.int32, (TOK, HD), 0) + position
        lane = lax.broadcasted_iota(jnp.int32, (TOK, HD), 1)
        late = jnp.where(key >= first, F32(0), F32(NEVER))
        bias = jnp.where(lane < 3, F32(1), jnp.where(lane == 3, late, F32(0)))
        k_ref[rows, HD:] = bias.astype(BF16)
    vt_ref[...] = jnp.concatenate([block[TOK:] for block, _ in blocks], 0).T


def pair(ours, theirs, step, side):
    return [(ours, step * TOK), (theirs, (step + side) * TOK)]


def partial(g, qt_ref, k_ref, vt_ref):
    p = jnp.exp2(dot(k_ref[...], qt_ref[:, columns(g)]) * SCALE)
    return dot(vt_ref[...], p.astype(BF16)), fold(p)


def first_keys(k_ref, vt_ref, blocks):
    keys = len(blocks) * TOK
    return k_ref.at[pl.ds(0, keys)], vt_ref.at[:, pl.ds(0, keys)]


def add_all(need, blocks, qt_ref, acc_in, tot_in, acc, tot, first, k_ref, vt_ref):
    @pl.when(need)
    def _():
        fill(blocks, first, k_ref, vt_ref)

        @pl.loop(0, GROUPS)
        def _(g):
            a, t = partial(g, qt_ref, k_ref, vt_ref)
            acc[:, columns(g)] = acc_in[:, columns(g)] + a
            tot[:, columns(g)] = tot_in[:, columns(g)] + t


def z_kernel(first_ref, qt_ref, z, z2, acc_in, tot_in, acc, tot, k_ref, vt_ref):
    _, core = place()
    first = first_ref[0]
    blocks = pair(z, z2, -8, 1 - 2 * core)
    add_all(first < -6 * TOK, blocks, qt_ref, acc_in, tot_in, acc, tot, first, k_ref, vt_ref)


def near_kernel(first_ref, qt_ref, n1, n3, mx, acc_in, tot_in, acc, tot, k_ref, vt_ref):
    _, core = place()
    first = first_ref[0]
    side = 1 - 2 * core
    blocks = pair(n1, mx.at[NEW], -2, side) + pair(n3, mx.at[OLD], -6, side)
    some = first < -4 * TOK
    state = (qt_ref, acc_in, tot_in, acc, tot, first)
    add_all(some, blocks, *state, k_ref, vt_ref)
    few = jnp.logical_not(some) & (first < 0)
    add_all(few, blocks[:2], *state, *first_keys(k_ref, vt_ref, blocks[:2]))


def far_kernel(
    first_ref, qt_ref, f1, f3, g, mx, acc_in, tot_in, acc, tot, k_ref, vt_ref, k1_ref, vt1_ref
):
    _, core = place()
    first = first_ref[0]
    side = 1 - 2 * core
    blocks = pair(f1, g.at[NEW], -10, side) + pair(f3, g.at[OLD], -14, side)
    blocks.append((mx.at[THIRD], jnp.where(core == 0, -15, -1) * TOK))
    some = first < -8 * TOK
    state = (qt_ref, acc_in, tot_in, acc, tot, first)
    add_all(some, blocks, *state, k_ref, vt_ref)
    few = jnp.logical_not(some) & (core == 1) & (first < 0)
    add_all(few, blocks[4:], *state, k1_ref, vt1_ref)


def last_kernel(
    first_ref, qt_ref, r2, t2, n1, n3, mx, f1, f3, fo, z, z2, own, begin_ref, acc, tot,
    out_hbm, k_ref, vt_ref, out_ref, window, sems,
):
    _, core = place()
    side = 1 - 2 * core
    first = first_ref[0]
    blocks = pair(r2.at[NEW], t2.at[NEW], -4, side) + pair(r2.at[OLD], t2.at[OLD], -12, side)
    some = first < -10 * TOK
    few = jnp.logical_not(some) & (first < -2 * TOK)
    half = first_keys(k_ref, vt_ref, blocks[:2])

    @pl.when(some)
    def _():
        fill(blocks, first, k_ref, vt_ref)

    @pl.when(few)
    def _():
        fill(blocks[:2], first, *half)

    def send(g):
        return pltpu.make_async_copy(
            out_ref.at[lax.rem(g, 2)], out_hbm.at[:, columns(g, GROUP * HD)], sems.at[lax.rem(g, 2)]
        )

    def put(g, result):
        result = result.astype(BF16)
        for i in range(GROUP):
            part = result[:, i * TOK : (i + 1) * TOK].T
            out_ref[lax.rem(g, 2), :, i * HD : (i + 1) * HD] = part

    @pl.loop(0, GROUPS)
    def _(g):
        @pl.when(g >= 2)
        def _():
            send(g - 2).wait()

        def finish(a, t):
            total = jnp.sum(t, 0, keepdims=True)
            put(g, a / total)
            return jnp.max(total)

        def with_blocks(refs):
            a, t = partial(g, qt_ref, *refs)
            return finish(acc[:, columns(g)] + a, tot[:, columns(g)] + t)

        def without():
            return finish(acc[:, columns(g)], tot[:, columns(g)])

        largest = lax.cond(
            some,
            lambda: with_blocks((k_ref, vt_ref)),
            lambda: lax.cond(few, lambda: with_blocks(half), without),
        )

        @pl.when(jnp.logical_not(largest < F32(1e30)))
        def _():
            pieces = [(own, 0), (z, -8), (z2, side - 8), (mx.at[THIRD], jnp.where(core == 0, -15, -1))]
            for i, ours, theirs in (
                (-2, n1, mx.at[NEW]), (-6, n3, mx.at[OLD]), (-10, f1, fo.at[NEW]), (-14, f3, fo.at[OLD]),
                (-4, r2.at[NEW], t2.at[NEW]), (-12, r2.at[OLD], t2.at[OLD]),
            ):
                pieces += [(ours, i), (theirs, i + side)]
            for piece, step in pieces:
                window[step + 15] = piece[...]
            q = qt_ref[:HD, columns(g)]
            row = jnp.concatenate([lax.broadcasted_iota(jnp.int32, (1, TOK), 1)] * GROUP, 1)

            def step(i, carry):
                top, a, t = carry
                s = dot(window[15 - i, :TOK], q) * SCALE
                key = lax.broadcasted_iota(jnp.int32, (TOK, M), 0) - i * TOK
                keep = (key <= row) & (key >= begin_ref[...])
                s = jnp.where(keep, s, F32(NEVER))
                new = jnp.maximum(top, jnp.max(s, 0, keepdims=True))
                p = jnp.where(keep, jnp.exp2(s - new), F32(0))
                decay = jnp.exp2(top - new)
                return new, a * decay + dot(window[15 - i, TOK:].T, p.astype(BF16)), t * decay + fold(p)

            zero = (jnp.full((1, M), NEVER, F32), jnp.zeros((HD, M), F32), jnp.zeros((8, M), F32))
            _, a, t = lax.fori_loop(0, 16, step, zero)
            put(g, a / jnp.sum(t, 0, keepdims=True))

        send(g).start()

    for g in (GROUPS - 2, GROUPS - 1):
        send(g).wait()


VMEM = pl.BlockSpec(memory_space=pltpu.VMEM)
SMEM = pl.BlockSpec(memory_space=pltpu.SMEM)
ANY = pl.BlockSpec(memory_space=pl.ANY)
QT = pltpu.VMEM((2 * HD, HEADS * TOK), BF16)
ACC = pltpu.VMEM((HD, HEADS * TOK), F32)
TOT = pltpu.VMEM((8, HEADS * TOK), F32)


def params(mib):
    return pltpu.CompilerParams(vmem_limit_bytes=mib * MIB)


def cost(keys):
    rows = HEADS * TOK
    return pl.CostEstimate(
        flops=8 * rows * keys * HD, bytes_accessed=MIB, transcendentals=rows * keys
    )


def layout(keys):
    return [pltpu.VMEM((keys, 2 * HD), BF16), pltpu.VMEM((HD, keys), BF16)]


def chip(array):
    return pltpu.with_memory_space_constraint(array, pltpu.VMEM)


def smem(array):
    return pltpu.with_memory_space_constraint(array, pltpu.SMEM)


def hbm(array):
    return pltpu.with_memory_space_constraint(array, pltpu.HBM)


def permute(block, pairs):
    return lax.ppermute(block, AXES, pairs)


def shift_row(block):
    return permute(block, [(i, (i + ROW) % DEVICES) for i in range(DEVICES)])


def swap(block):
    return permute(block, [(i, i ^ 1) for i in range(DEVICES)])


def pack(keys, values):
    return pl.pallas_call(
        pack_kernel,
        out_shape=pltpu.VMEM((2 * TOK, HD), BF16),
        in_specs=[ANY, ANY],
        out_specs=VMEM,
        scratch_shapes=[pltpu.SemaphoreType.DMA((2,))],
        compiler_params=params(4),
        name="pack",
    )(hbm(keys), hbm(values))


def own_part(queries, own, doc_lengths):
    return pl.pallas_call(
        own_kernel,
        out_shape=(
            QT, ACC, TOT, pltpu.VMEM((1, M), jnp.int32), pltpu.SMEM((1,), jnp.int32)
        ),
        in_specs=[ANY, ANY, VMEM],
        out_specs=(VMEM, VMEM, VMEM, VMEM, SMEM),
        scratch_shapes=[
            pltpu.VMEM((TOK, M), F32),
            pltpu.VMEM(queries.shape, BF16),
            pltpu.SMEM((NDOCS,), jnp.int32),
            pltpu.SemaphoreType.DMA((GROUPS,)),
            pltpu.SemaphoreType.DMA,
        ],
        compiler_params=params(24),
        cost_estimate=cost(TOK),
        name="own",
    )(hbm(doc_lengths), hbm(queries), chip(own))


def add_part(kernel, name, keys, first, qt, blocks, acc, tot):
    at = 2 + len(blocks)
    return pl.pallas_call(
        kernel,
        out_shape=(ACC, TOT),
        in_specs=[SMEM] + [VMEM] * (3 + len(blocks)),
        out_specs=(VMEM, VMEM),
        scratch_shapes=layout(keys) + (layout(TOK) if name == "far" else []),
        input_output_aliases={at: 0, at + 1: 1},
        compiler_params=params(30),
        cost_estimate=cost(keys),
        name=name,
    )(smem(first), *[chip(a) for a in (qt, *blocks, acc, tot)])


def last_part(first, arrays, shape):
    return pl.pallas_call(
        last_kernel,
        out_shape=jax.ShapeDtypeStruct(shape, BF16),
        in_specs=[SMEM] + [VMEM] * len(arrays),
        out_specs=pl.BlockSpec(memory_space=pl.ANY),
        scratch_shapes=layout(4 * TOK)
        + [
            pltpu.VMEM((2, TOK, GROUP * HD), BF16),
            pltpu.VMEM((16, 2 * TOK, HD), BF16),
            pltpu.SemaphoreType.DMA((2,)),
        ],
        compiler_params=params(36),
        cost_estimate=cost(4 * TOK),
        name="last",
    )(smem(first), *[chip(x) for x in arrays])


def shards(queries, keys, values, doc_lengths):
    col = lax.axis_index("inner") % ROW // 2
    own = pack(keys, values)

    def around(s, *pairs):
        behind = col + s < ROW // 2
        message = [jnp.where(behind, recent, older) for recent, older in pairs]
        route = [(i, i // ROW * ROW + (i + 2 * s) % ROW) for i in range(DEVICES)]
        return permute(jnp.concatenate(message, 0), route)

    z = shift_row(own)
    qt, acc, tot, begin, first = own_part(queries, own, doc_lengths)
    z, acc, tot = lax.optimization_barrier((z, acc, tot))

    n1, n3 = around(1, (own, z)), around(3, (own, z))
    zz = shift_row(z)
    z2 = swap(z)
    acc, tot = add_part(z_kernel, "zpart", 2 * TOK, first, qt, (z, z2), acc, tot)

    n1, n3, zz, tot = lax.optimization_barrier((n1, n3, zz, tot))
    f1, f3 = around(1, (z, zz)), around(3, (z, zz))
    r2 = around(2, (own, z), (z, zz))
    x = jnp.where(lax.axis_index("inner") % 2 == 0, own, zz)
    mx = swap(jnp.concatenate([n1, n3, x], 0))
    acc, tot = add_part(near_kernel, "near", 4 * TOK, first, qt, (n1, n3, mx), acc, tot)

    f1, f3, tot = lax.optimization_barrier((f1, f3, tot))
    g = swap(jnp.concatenate([f1, f3], 0))
    acc, tot = add_part(far_kernel, "far", 5 * TOK, first, qt, (f1, f3, g, mx), acc, tot)

    r2, tot = lax.optimization_barrier((r2, tot))
    t2 = swap(r2)
    arrays = (qt, r2, t2, n1, n3, mx, f1, f3, g, z, z2, own, begin, acc, tot)
    return last_part(first, arrays, queries.shape)


def solution(mesh):
    rows = P(AXES, None)
    return jax.shard_map(
        shards, mesh=mesh, in_specs=(rows, rows, rows, P()), out_specs=rows, check_vma=False
    )
```

profile of v0, /device:TPU:1, one launch (start us, length us, event | category | flops | bytes accessed | tf_op | source)
XLA Modules:
  0.0 49.0 jit_solution(4919904904069517044)
XLA Ops:
  0.0 0.9 %pack.1.kv_ref.own = bf16[640,128]{1,0:T(8,128)(2,1)S(1)} custom-call(bf16[320,128]{1,0:T(8,128)(2,1)} %k_hbm.1, bf16[320,128]{1,0:T(8,128)(2,1)} %v_hbm.1), custom_call_target="tpu_custom_call" | custom-call | tf_op jit(solution)/shard_map/pack/pallas_call | solution.py:325
  1.0 2.5 %collective-permute-start = (bf16[640,128]{1,0:T(8,128)(2,1)S(1)}, bf16[640,128]{1,0:T(8,128)(2,1)S(1)}, u32[]{:S(2)}, u32[]{:S(2)}) collective-permute-start(bf16[640,128]{1,0:T(8,128)(2,1)S(1)} %pack.1.kv_ref.own), channel_id=1, source_target_pairs={{0,8},{1,9},{2,10},{3,11},{4,12},{5,13},{6,14},{7,15},{8,16},{9,17... | collective-permute-start | bytes 491528 | tf_op jit(solution)/shard_map/ppermute | solution.py:313
  3.5 4.4 %own.1 = (bf16[256,5120]{1,0:T(8,128)(2,1)S(1)}, f32[128,5120]{1,0:T(8,128)S(1)}, f32[8,5120]{1,0:T(8,128)S(1)}, s32[1,2560]{1,0:T(1,128)S(1)}, s32[1]{0:T(128)S(4)}) custom-call(s32[64]{0:T(128)} %docs_hbm.1, bf16[320,2048]{1,0:T(8,128)(2,1)} %q_hbm.1, bf16[640,128]{1,0:T(8,128)(2,1)S(1)} %pack.1.kv_ref.own), custom_call_target="tpu_custom_call" | custom-call | flops 1677721600 | bytes 1048576 | tf_op jit(solution)/shard_map/own/pallas_call | solution.py:337
  7.9 4.0 %collective-permute-done.z = bf16[640,128]{1,0:T(8,128)(2,1)S(1)} collective-permute-done((bf16[640,128]{1,0:T(8,128)(2,1)S(1)}, bf16[640,128]{1,0:T(8,128)(2,1)S(1)}, u32[]{:S(2)}, u32[]{:S(2)}) %collective-permute-start) | collective-permute-done | bytes 163872 | tf_op jit(solution)/shard_map/ppermute | solution.py:313
  12.0 1.2 %collective-permute-start.4 = (bf16[640,128]{1,0:T(8,128)(2,1)S(1)}, bf16[640,128]{1,0:T(8,128)(2,1)S(1)}, u32[]{:S(2)}, u32[]{:S(2)}) collective-permute-start(bf16[640,128]{1,0:T(8,128)(2,1)S(1)} %collective-permute-done.z), channel_id=1, source_target_pairs={{0,1},{1,0},{2,3},{3,2},{4,5},{5,4},{6,7},{7,6},{8,9},{9,8},{10,11... | collective-permute-start | bytes 491528 | tf_op jit(solution)/shard_map/ppermute | solution.py:313
  13.2 0.0 collective-permute-start.3
  13.3 2.5 %collective-permute-start.2 = (bf16[640,128]{1,0:T(8,128)(2,1)S(1)}, bf16[640,128]{1,0:T(8,128)(2,1)S(1)}, u32[]{:S(2)}, u32[]{:S(2)}) collective-permute-start(bf16[640,128]{1,0:T(8,128)(2,1)S(1)} %get-tuple-element.55), channel_id=1, source_target_pairs={{0,6},{1,7},{2,0},{3,1},{4,2},{5,3},{6,4},{7,5},{8,14},{9,15},{10,... | collective-permute-start | bytes 491528 | tf_op jit(solution)/shard_map/ppermute | solution.py:313
  15.8 0.0 collective-permute-start.1
  15.8 0.0 collective-permute-done.4.z2
  15.8 6.6 %collective-permute-done.3 = bf16[640,128]{1,0:T(8,128)(2,1)S(1)} collective-permute-done((bf16[640,128]{1,0:T(8,128)(2,1)S(1)}, bf16[640,128]{1,0:T(8,128)(2,1)S(1)}, u32[]{:S(2)}, u32[]{:S(2)}) %collective-permute-start.3) | collective-permute-done | bytes 163872 | tf_op jit(solution)/shard_map/ppermute | solution.py:313
  22.4 0.0 collective-permute-done.2.n3
  22.4 0.2 collective-permute-done.1.n1
  22.5 0.1 broadcast_select_fusion.1
  22.6 1.2 %collective-permute-start.8 = (bf16[1920,128]{1,0:T(8,128)(2,1)S(1)}, bf16[1920,128]{1,0:T(8,128)(2,1)S(1)}, u32[]{:S(2)}, u32[]{:S(2)}) collective-permute-start(bf16[1920,128]{1,0:T(8,128)(2,1)S(1)} %pad_maximum_fusion), channel_id=1, source_target_pairs={{0,1},{1,0},{2,3},{3,2},{4,5},{5,4},{6,7},{7,6},{8,9},{9,8},{10,11... | collective-permute-start | bytes 1474568 | tf_op jit(solution)/shard_map/ppermute | solution.py:313
  23.8 2.0 %collective-permute-start.7 = (bf16[640,128]{1,0:T(8,128)(2,1)S(1)}, bf16[640,128]{1,0:T(8,128)(2,1)S(1)}, u32[]{:S(2)}, u32[]{:S(2)}) collective-permute-start(bf16[640,128]{1,0:T(8,128)(2,1)S(1)} %get-tuple-element.51), channel_id=1, source_target_pairs={{0,6},{1,7},{2,0},{3,1},{4,2},{5,3},{6,4},{7,5},{8,14},{9,15},{10,... | collective-permute-start | bytes 491528 | tf_op jit(solution)/shard_map/ppermute | solution.py:313
  25.8 0.0 collective-permute-start.6
  25.8 0.0 collective-permute-done.8.mx
  25.8 3.4 %near.1 = (f32[128,5120]{1,0:T(8,128)S(1)}, f32[8,5120]{1,0:T(8,128)S(1)}) custom-call(s32[1]{0:T(128)S(4)} %get-tuple-element.28.first_ref, bf16[256,5120]{1,0:T(8,128)(2,1)S(1)} %get-tuple-element.29.qt_ref, bf16[640,128]{1,0:T(8,128)(2,1)S(1)} %collective-permute-done.1.n1, ...), custom_call_target="tpu_custom_call", output_to_operand_aliasing={{0}: (5, {}), {1}: (6, {})} | custom-call | flops 6710886400 | bytes 1048576 | tf_op jit(solution)/shard_map/near/pallas_call | solution.py:359
  29.2 0.3 collective-permute-done.7.f3
  29.6 2.9 %collective-permute-done.6.f1 = bf16[640,128]{1,0:T(8,128)(2,1)S(1)} collective-permute-done((bf16[640,128]{1,0:T(8,128)(2,1)S(1)}, bf16[640,128]{1,0:T(8,128)(2,1)S(1)}, u32[]{:S(2)}, u32[]{:S(2)}) %collective-permute-start.6) | collective-permute-done | bytes 163872 | tf_op jit(solution)/shard_map/ppermute | solution.py:313
  32.5 1.3 %collective-permute-start.9 = (bf16[1280,128]{1,0:T(8,128)(2,1)S(1)}, bf16[1280,128]{1,0:T(8,128)(2,1)S(1)}, u32[]{:S(2)}, u32[]{:S(2)}) collective-permute-start(bf16[1280,128]{1,0:T(8,128)(2,1)S(1)} %pad_maximum_fusion.2), channel_id=1, source_target_pairs={{0,1},{1,0},{2,3},{3,2},{4,5},{5,4},{6,7},{7,6},{8,9},{9,8},{10,11... | collective-permute-start | bytes 983048 | tf_op jit(solution)/shard_map/ppermute | solution.py:313
  33.8 0.1 collective-permute-start.5
  33.9 1.1 %collective-permute-done.9.g.fo = bf16[1280,128]{1,0:T(8,128)(2,1)S(1)} collective-permute-done((bf16[1280,128]{1,0:T(8,128)(2,1)S(1)}, bf16[1280,128]{1,0:T(8,128)(2,1)S(1)}, u32[]{:S(2)}, u32[]{:S(2)}) %collective-permute-start.9) | collective-permute-done | bytes 327712 | tf_op jit(solution)/shard_map/ppermute | solution.py:313
  35.0 2.2 %far.1 = (f32[128,5120]{1,0:T(8,128)S(1)}, f32[8,5120]{1,0:T(8,128)S(1)}) custom-call(s32[1]{0:T(128)S(4)} %get-tuple-element.28.first_ref, bf16[256,5120]{1,0:T(8,128)(2,1)S(1)} %get-tuple-element.29.qt_ref, bf16[640,128]{1,0:T(8,128)(2,1)S(1)} %collective-permute-done.6.f1, ...), custom_call_target="tpu_custom_call", output_to_operand_aliasing={{0}: (6, {}), {1}: (7, {})} | custom-call | flops 8388608000 | bytes 1048576 | tf_op jit(solution)/shard_map/far/pallas_call | solution.py:359
  37.2 7.5 %collective-permute-done.5.r2 = bf16[1280,128]{1,0:T(8,128)(2,1)S(1)} collective-permute-done((bf16[1280,128]{1,0:T(8,128)(2,1)S(1)}, bf16[1280,128]{1,0:T(8,128)(2,1)S(1)}, u32[]{:S(2)}, u32[]{:S(2)}) %collective-permute-start.5) | collective-permute-done | bytes 327712 | tf_op jit(solution)/shard_map/ppermute | solution.py:313
  44.7 0.8 %collective-permute-start.10 = (bf16[1280,128]{1,0:T(8,128)(2,1)S(1)}, bf16[1280,128]{1,0:T(8,128)(2,1)S(1)}, u32[]{:S(2)}, u32[]{:S(2)}) collective-permute-start(bf16[1280,128]{1,0:T(8,128)(2,1)S(1)} %collective-permute-done.5.r2), channel_id=1, source_target_pairs={{0,1},{1,0},{2,3},{3,2},{4,5},{5,4},{6,7},{7,6},{8,9},{9,8},{10,11... | collective-permute-start | bytes 983048 | tf_op jit(solution)/shard_map/ppermute | solution.py:313
  45.5 1.3 %collective-permute-done.10.t2 = bf16[1280,128]{1,0:T(8,128)(2,1)S(1)} collective-permute-done((bf16[1280,128]{1,0:T(8,128)(2,1)S(1)}, bf16[1280,128]{1,0:T(8,128)(2,1)S(1)}, u32[]{:S(2)}, u32[]{:S(2)}) %collective-permute-start.10) | collective-permute-done | bytes 327712 | tf_op jit(solution)/shard_map/ppermute | solution.py:313
  46.7 2.1 %last.1 = bf16[320,2048]{1,0:T(8,128)(2,1)} custom-call(s32[1]{0:T(128)S(4)} %get-tuple-element.28.first_ref, bf16[256,5120]{1,0:T(8,128)(2,1)S(1)} %get-tuple-element.29.qt_ref, bf16[1280,128]{1,0:T(8,128)(2,1)S(1)} %collective-permute-done.5.r2, bf16[1280,128]{1,0:T(8,128)(2,1)S(1)} %collective-permute-done.10.t2, ...), custom_call_target="tpu_custom_call" | custom-call | flops 6710886400 | bytes 1048576 | tf_op jit(solution)/shard_map/last/pallas_call | solution.py:373
  (5 shorter events, 0.1 us)
Async XLA Ops:
  1.0 11.0 %collective-permute-start = (bf16[640,128]{1,0:T(8,128)(2,1)S(1)}, bf16[640,128]{1,0:T(8,128)(2,1)S(1)}, u32[]{:S(2)}, u32[]{:S(2)}) collective-permute-start(bf16[640,128]{1,0:T(8,128)(2,1)S(1)} %pack.1.kv_ref.own), channel_id=1, source_target_pairs={{0,8},{1,9},{2,10},{3,11},{4,12},{5,13},{6,14},{7,15},{8,16},{9,17... | collective-permute-start | bytes 491528 | tf_op jit(solution)/shard_map/ppermute | solution.py:313
  12.0 3.8 %collective-permute-start.4 = (bf16[640,128]{1,0:T(8,128)(2,1)S(1)}, bf16[640,128]{1,0:T(8,128)(2,1)S(1)}, u32[]{:S(2)}, u32[]{:S(2)}) collective-permute-start(bf16[640,128]{1,0:T(8,128)(2,1)S(1)} %collective-permute-done.z), channel_id=1, source_target_pairs={{0,1},{1,0},{2,3},{3,2},{4,5},{5,4},{6,7},{7,6},{8,9},{9,8},{10,11... | collective-permute-start | bytes 491528 | tf_op jit(solution)/shard_map/ppermute | solution.py:313
  13.2 9.2 %collective-permute-start.3 = (bf16[640,128]{1,0:T(8,128)(2,1)S(1)}, bf16[640,128]{1,0:T(8,128)(2,1)S(1)}, u32[]{:S(2)}, u32[]{:S(2)}) collective-permute-start(bf16[640,128]{1,0:T(8,128)(2,1)S(1)} %collective-permute-done.z), channel_id=1, source_target_pairs={{0,8},{1,9},{2,10},{3,11},{4,12},{5,13},{6,14},{7,15},{8,16},{9,17... | collective-permute-start | bytes 491528 | tf_op jit(solution)/shard_map/ppermute | solution.py:313
  13.3 9.1 %collective-permute-start.2 = (bf16[640,128]{1,0:T(8,128)(2,1)S(1)}, bf16[640,128]{1,0:T(8,128)(2,1)S(1)}, u32[]{:S(2)}, u32[]{:S(2)}) collective-permute-start(bf16[640,128]{1,0:T(8,128)(2,1)S(1)} %get-tuple-element.55), channel_id=1, source_target_pairs={{0,6},{1,7},{2,0},{3,1},{4,2},{5,3},{6,4},{7,5},{8,14},{9,15},{10,... | collective-permute-start | bytes 491528 | tf_op jit(solution)/shard_map/ppermute | solution.py:313
  15.8 6.7 %collective-permute-start.1 = (bf16[640,128]{1,0:T(8,128)(2,1)S(1)}, bf16[640,128]{1,0:T(8,128)(2,1)S(1)}, u32[]{:S(2)}, u32[]{:S(2)}) collective-permute-start(bf16[640,128]{1,0:T(8,128)(2,1)S(1)} %get-tuple-element.56), channel_id=1, source_target_pairs={{0,2},{1,3},{2,4},{3,5},{4,6},{5,7},{6,0},{7,1},{8,10},{9,11},{10,... | collective-permute-start | bytes 491528 | tf_op jit(solution)/shard_map/ppermute | solution.py:313
  22.6 3.2 %collective-permute-start.8 = (bf16[1920,128]{1,0:T(8,128)(2,1)S(1)}, bf16[1920,128]{1,0:T(8,128)(2,1)S(1)}, u32[]{:S(2)}, u32[]{:S(2)}) collective-permute-start(bf16[1920,128]{1,0:T(8,128)(2,1)S(1)} %pad_maximum_fusion), channel_id=1, source_target_pairs={{0,1},{1,0},{2,3},{3,2},{4,5},{5,4},{6,7},{7,6},{8,9},{9,8},{10,11... | collective-permute-start | bytes 1474568 | tf_op jit(solution)/shard_map/ppermute | solution.py:313
  23.8 5.8 %collective-permute-start.7 = (bf16[640,128]{1,0:T(8,128)(2,1)S(1)}, bf16[640,128]{1,0:T(8,128)(2,1)S(1)}, u32[]{:S(2)}, u32[]{:S(2)}) collective-permute-start(bf16[640,128]{1,0:T(8,128)(2,1)S(1)} %get-tuple-element.51), channel_id=1, source_target_pairs={{0,6},{1,7},{2,0},{3,1},{4,2},{5,3},{6,4},{7,5},{8,14},{9,15},{10,... | collective-permute-start | bytes 491528 | tf_op jit(solution)/shard_map/ppermute | solution.py:313
  25.8 6.6 %collective-permute-start.6 = (bf16[640,128]{1,0:T(8,128)(2,1)S(1)}, bf16[640,128]{1,0:T(8,128)(2,1)S(1)}, u32[]{:S(2)}, u32[]{:S(2)}) collective-permute-start(bf16[640,128]{1,0:T(8,128)(2,1)S(1)} %get-tuple-element.52), channel_id=1, source_target_pairs={{0,2},{1,3},{2,4},{3,5},{4,6},{5,7},{6,0},{7,1},{8,10},{9,11},{10,... | collective-permute-start | bytes 491528 | tf_op jit(solution)/shard_map/ppermute | solution.py:313
  32.5 2.5 %collective-permute-start.9 = (bf16[1280,128]{1,0:T(8,128)(2,1)S(1)}, bf16[1280,128]{1,0:T(8,128)(2,1)S(1)}, u32[]{:S(2)}, u32[]{:S(2)}) collective-permute-start(bf16[1280,128]{1,0:T(8,128)(2,1)S(1)} %pad_maximum_fusion.2), channel_id=1, source_target_pairs={{0,1},{1,0},{2,3},{3,2},{4,5},{5,4},{6,7},{7,6},{8,9},{9,8},{10,11... | collective-permute-start | bytes 983048 | tf_op jit(solution)/shard_map/ppermute | solution.py:313
  33.8 10.9 %collective-permute-start.5 = (bf16[1280,128]{1,0:T(8,128)(2,1)S(1)}, bf16[1280,128]{1,0:T(8,128)(2,1)S(1)}, u32[]{:S(2)}, u32[]{:S(2)}) collective-permute-start(bf16[1280,128]{1,0:T(8,128)(2,1)S(1)} %pad_maximum_fusion.1), channel_id=1, source_target_pairs={{0,4},{1,5},{2,6},{3,7},{4,0},{5,1},{6,2},{7,3},{8,12},{9,13},{10,... | collective-permute-start | bytes 983048 | tf_op jit(solution)/shard_map/ppermute | solution.py:313
  44.7 2.1 %collective-permute-start.10 = (bf16[1280,128]{1,0:T(8,128)(2,1)S(1)}, bf16[1280,128]{1,0:T(8,128)(2,1)S(1)}, u32[]{:S(2)}, u32[]{:S(2)}) collective-permute-start(bf16[1280,128]{1,0:T(8,128)(2,1)S(1)} %collective-permute-done.5.r2), channel_id=1, source_target_pairs={{0,1},{1,0},{2,3},{3,2},{4,5},{5,4},{6,7},{7,6},{8,9},{9,8},{10,11... | collective-permute-start | bytes 983048 | tf_op jit(solution)/shard_map/ppermute | solution.py:313
where the time goes:
time: 49.9 us; the launch traced here: 49 us
  waiting for transfers between devices  23.9 us (48%)
  Pallas kernels  13 us (26%)
  starting transfers between devices  11.7 us (23%)
    ppermute x11, waiting for transfers between devices, permute(): return lax.ppermute(block, AXES, pairs)  23.9 us
    ppermute x11, starting transfers between devices, permute(): return lax.ppermute(block, AXES, pairs)  11.7 us
    pallas_call x3, Pallas kernels, add_part(): pl.pallas_call(kernel, out_shape=(ACC, TOT), in_specs=[SMEM] + [VMEM] * (...  5.57 us
    pallas_call x1, Pallas kernels, own_part(): pl.pallas_call(own_kernel, out_shape=(QT, ACC, TOT, pltpu.VMEM((1, M), jn...  4.44 us
    pallas_call x1, Pallas kernels, last_part(): pl.pallas_call(last_kernel, out_shape=jax.ShapeDtypeStruct(shape, BF16),...  2.1 us
  transfers between devices with their start and end apart: 11, of which 8 were waited for; matrix products, arithmetic and copies ran while one was open for 0% of the time, Pallas kernels for 20%

commit v1 on v0

--- a/solution.py
+++ b/solution.py
@@ -162,7 +162,7 @@
     _, core = place()
     first = first_ref[0]
     side = 1 - 2 * core
-    blocks = pair(n1, mx.at[NEW], -2, side) + pair(n3, mx.at[OLD], -6, side)
+    blocks = pair(n1, mx.at[NEW], -2, side) + [(n3, -6 * TOK)]
     some = first < -4 * TOK
     state = (qt_ref, acc_in, tot_in, acc, tot, first)
     add_all(some, blocks, *state, k_ref, vt_ref)
@@ -177,11 +177,12 @@
     first = first_ref[0]
     side = 1 - 2 * core
     blocks = pair(f1, g.at[NEW], -10, side) + pair(f3, g.at[OLD], -14, side)
+    blocks.append((mx.at[OLD], (side - 6) * TOK))
     blocks.append((mx.at[THIRD], jnp.where(core == 0, -15, -1) * TOK))
     some = first < -8 * TOK
     state = (qt_ref, acc_in, tot_in, acc, tot, first)
     add_all(some, blocks, *state, k_ref, vt_ref)
-    few = jnp.logical_not(some) & (core == 1) & (first < 0)
+    few = jnp.logical_not(some) & (first < jnp.where(core == 1, 0, -4) * TOK)
     add_all(few, blocks[4:], *state, k1_ref, vt1_ref)
 
 
@@ -361,9 +362,9 @@
         out_shape=(ACC, TOT),
         in_specs=[SMEM] + [VMEM] * (3 + len(blocks)),
         out_specs=(VMEM, VMEM),
-        scratch_shapes=layout(keys) + (layout(TOK) if name == "far" else []),
+        scratch_shapes=layout(keys) + (layout(2 * TOK) if name == "far" else []),
         input_output_aliases={at: 0, at + 1: 1},
-        compiler_params=params(30),
+        compiler_params=params(36),
         cost_estimate=cost(keys),
         name=name,
     )(smem(first), *[chip(a) for a in (qt, *blocks, acc, tot)])
@@ -411,11 +412,11 @@
     r2 = around(2, (own, z), (z, zz))
     x = jnp.where(lax.axis_index("inner") % 2 == 0, own, zz)
     mx = swap(jnp.concatenate([n1, n3, x], 0))
-    acc, tot = add_part(near_kernel, "near", 4 * TOK, first, qt, (n1, n3, mx), acc, tot)
+    acc, tot = add_part(near_kernel, "near", 3 * TOK, first, qt, (n1, n3, mx), acc, tot)
 
     f1, f3, tot = lax.optimization_barrier((f1, f3, tot))
     g = swap(jnp.concatenate([f1, f3], 0))
-    acc, tot = add_part(far_kernel, "far", 5 * TOK, first, qt, (f1, f3, g, mx), acc, tot)
+    acc, tot = add_part(far_kernel, "far", 6 * TOK, first, qt, (f1, f3, g, mx), acc, tot)
 
     r2, tot = lax.optimization_barrier((r2, tot))
     t2 = swap(r2)

time: 49.9 us -> 49.7 us (level)
  Pallas kernels: 13 us -> 14.3 us
  waiting for transfers between devices: 23.9 us -> 22.6 us
    pallas_call x3, Pallas kernels: 5.57 us -> 6.82 us  [add_part(): pl.pallas_call(kernel, out_shape=(ACC, TOT), in_specs=[SMEM] + [VMEM] * (...]
    ppermute x11, waiting for transfers between devices: 23.9 us -> 22.6 us  [permute(): return lax.ppermute(block, AXES, pairs)]
  transfers between devices with their start and end apart: 11 -> 11, of which waited for: 8 -> 8; matrix products, arithmetic and copies ran while one was open for 0% -> 0% of each run, Pallas kernels for 20% -> 23%
where the time goes in v1:
time: 49.7 us; the launch traced here: 49 us
  waiting for transfers between devices  22.6 us (45%)
  Pallas kernels  14.3 us (29%)
  starting transfers between devices  11.7 us (24%)
    ppermute x11, waiting for transfers between devices, permute(): return lax.ppermute(block, AXES, pairs)  22.6 us
    ppermute x11, starting transfers between devices, permute(): return lax.ppermute(block, AXES, pairs)  11.7 us
    pallas_call x3, Pallas kernels, add_part(): pl.pallas_call(kernel, out_shape=(ACC, TOT), in_specs=[SMEM] + [VMEM] * (...  6.82 us
    pallas_call x1, Pallas kernels, own_part(): pl.pallas_call(own_kernel, out_shape=(QT, ACC, TOT, pltpu.VMEM((1, M), jn...  4.44 us
    pallas_call x1, Pallas kernels, last_part(): pl.pallas_call(last_kernel, out_shape=jax.ShapeDtypeStruct(shape, BF16),...  2.1 us
  transfers between devices with their start and end apart: 11, of which 8 were waited for; matrix products, arithmetic and copies ran while one was open for 0% of the time, Pallas kernels for 23%

profile of v1, /device:TPU:1, one launch (start us, length us, event | category | flops | bytes accessed | tf_op | source)
XLA Modules:
  0.0 49.0 jit_solution(7432965527340936897)
XLA Ops:
  0.0 0.9 %pack.1.kv_ref.own = bf16[640,128]{1,0:T(8,128)(2,1)S(1)} custom-call(bf16[320,128]{1,0:T(8,128)(2,1)} %k_hbm.1, bf16[320,128]{1,0:T(8,128)(2,1)} %v_hbm.1), custom_call_target="tpu_custom_call" | custom-call | tf_op jit(solution)/shard_map/pack/pallas_call | solution.py:326
  1.0 2.5 %collective-permute-start = (bf16[640,128]{1,0:T(8,128)(2,1)S(1)}, bf16[640,128]{1,0:T(8,128)(2,1)S(1)}, u32[]{:S(2)}, u32[]{:S(2)}) collective-permute-start(bf16[640,128]{1,0:T(8,128)(2,1)S(1)} %pack.1.kv_ref.own), channel_id=1, source_target_pairs={{0,8},{1,9},{2,10},{3,11},{4,12},{5,13},{6,14},{7,15},{8,16},{9,17... | collective-permute-start | bytes 491528 | tf_op jit(solution)/shard_map/ppermute | solution.py:314
  3.5 4.4 %own.1 = (bf16[256,5120]{1,0:T(8,128)(2,1)S(1)}, f32[128,5120]{1,0:T(8,128)S(1)}, f32[8,5120]{1,0:T(8,128)S(1)}, s32[1,2560]{1,0:T(1,128)S(1)}, s32[1]{0:T(128)S(4)}) custom-call(s32[64]{0:T(128)} %docs_hbm.1, bf16[320,2048]{1,0:T(8,128)(2,1)} %q_hbm.1, bf16[640,128]{1,0:T(8,128)(2,1)S(1)} %pack.1.kv_ref.own), custom_call_target="tpu_custom_call" | custom-call | flops 1677721600 | bytes 1048576 | tf_op jit(solution)/shard_map/own/pallas_call | solution.py:338
  7.9 4.0 %collective-permute-done.z = bf16[640,128]{1,0:T(8,128)(2,1)S(1)} collective-permute-done((bf16[640,128]{1,0:T(8,128)(2,1)S(1)}, bf16[640,128]{1,0:T(8,128)(2,1)S(1)}, u32[]{:S(2)}, u32[]{:S(2)}) %collective-permute-start) | collective-permute-done | bytes 163872 | tf_op jit(solution)/shard_map/ppermute | solution.py:314
  12.0 1.2 %collective-permute-start.4 = (bf16[640,128]{1,0:T(8,128)(2,1)S(1)}, bf16[640,128]{1,0:T(8,128)(2,1)S(1)}, u32[]{:S(2)}, u32[]{:S(2)}) collective-permute-start(bf16[640,128]{1,0:T(8,128)(2,1)S(1)} %collective-permute-done.z), channel_id=1, source_target_pairs={{0,1},{1,0},{2,3},{3,2},{4,5},{5,4},{6,7},{7,6},{8,9},{9,8},{10,11... | collective-permute-start | bytes 491528 | tf_op jit(solution)/shard_map/ppermute | solution.py:314
  13.2 0.0 collective-permute-start.3
  13.3 2.5 %collective-permute-start.2 = (bf16[640,128]{1,0:T(8,128)(2,1)S(1)}, bf16[640,128]{1,0:T(8,128)(2,1)S(1)}, u32[]{:S(2)}, u32[]{:S(2)}) collective-permute-start(bf16[640,128]{1,0:T(8,128)(2,1)S(1)} %get-tuple-element.55), channel_id=1, source_target_pairs={{0,6},{1,7},{2,0},{3,1},{4,2},{5,3},{6,4},{7,5},{8,14},{9,15},{10,... | collective-permute-start | bytes 491528 | tf_op jit(solution)/shard_map/ppermute | solution.py:314
  15.8 0.0 collective-permute-start.1
  15.8 0.0 collective-permute-done.4.z2
  15.8 6.6 %collective-permute-done.3 = bf16[640,128]{1,0:T(8,128)(2,1)S(1)} collective-permute-done((bf16[640,128]{1,0:T(8,128)(2,1)S(1)}, bf16[640,128]{1,0:T(8,128)(2,1)S(1)}, u32[]{:S(2)}, u32[]{:S(2)}) %collective-permute-start.3) | collective-permute-done | bytes 163872 | tf_op jit(solution)/shard_map/ppermute | solution.py:314
  22.4 0.0 collective-permute-done.2.n3
  22.4 0.2 collective-permute-done.1.n1
  22.5 0.1 broadcast_select_fusion.1
  22.6 1.2 %collective-permute-start.8 = (bf16[1920,128]{1,0:T(8,128)(2,1)S(1)}, bf16[1920,128]{1,0:T(8,128)(2,1)S(1)}, u32[]{:S(2)}, u32[]{:S(2)}) collective-permute-start(bf16[1920,128]{1,0:T(8,128)(2,1)S(1)} %pad_maximum_fusion), channel_id=1, source_target_pairs={{0,1},{1,0},{2,3},{3,2},{4,5},{5,4},{6,7},{7,6},{8,9},{9,8},{10,11... | collective-permute-start | bytes 1474568 | tf_op jit(solution)/shard_map/ppermute | solution.py:314
  23.8 2.0 %collective-permute-start.7 = (bf16[640,128]{1,0:T(8,128)(2,1)S(1)}, bf16[640,128]{1,0:T(8,128)(2,1)S(1)}, u32[]{:S(2)}, u32[]{:S(2)}) collective-permute-start(bf16[640,128]{1,0:T(8,128)(2,1)S(1)} %get-tuple-element.51), channel_id=1, source_target_pairs={{0,6},{1,7},{2,0},{3,1},{4,2},{5,3},{6,4},{7,5},{8,14},{9,15},{10,... | collective-permute-start | bytes 491528 | tf_op jit(solution)/shard_map/ppermute | solution.py:314
  25.8 0.0 collective-permute-start.6
  25.8 0.0 collective-permute-done.8.mx
  25.8 3.4 %near.1 = (f32[128,5120]{1,0:T(8,128)S(1)}, f32[8,5120]{1,0:T(8,128)S(1)}) custom-call(s32[1]{0:T(128)S(4)} %get-tuple-element.28.first_ref, bf16[256,5120]{1,0:T(8,128)(2,1)S(1)} %get-tuple-element.29.qt_ref, bf16[640,128]{1,0:T(8,128)(2,1)S(1)} %collective-permute-done.1.n1, ...), custom_call_target="tpu_custom_call", output_to_operand_aliasing={{0}: (5, {}), {1}: (6, {})} | custom-call | flops 5033164800 | bytes 1048576 | tf_op jit(solution)/shard_map/near/pallas_call | solution.py:360
  29.2 0.3 collective-permute-done.7.f3
  29.6 2.9 %collective-permute-done.6.f1 = bf16[640,128]{1,0:T(8,128)(2,1)S(1)} collective-permute-done((bf16[640,128]{1,0:T(8,128)(2,1)S(1)}, bf16[640,128]{1,0:T(8,128)(2,1)S(1)}, u32[]{:S(2)}, u32[]{:S(2)}) %collective-permute-start.6) | collective-permute-done | bytes 163872 | tf_op jit(solution)/shard_map/ppermute | solution.py:314
  32.5 1.3 %collective-permute-start.9 = (bf16[1280,128]{1,0:T(8,128)(2,1)S(1)}, bf16[1280,128]{1,0:T(8,128)(2,1)S(1)}, u32[]{:S(2)}, u32[]{:S(2)}) collective-permute-start(bf16[1280,128]{1,0:T(8,128)(2,1)S(1)} %pad_maximum_fusion.2), channel_id=1, source_target_pairs={{0,1},{1,0},{2,3},{3,2},{4,5},{5,4},{6,7},{7,6},{8,9},{9,8},{10,11... | collective-permute-start | bytes 983048 | tf_op jit(solution)/shard_map/ppermute | solution.py:314
  33.8 0.1 collective-permute-start.5
  33.9 1.1 %collective-permute-done.9.g.fo = bf16[1280,128]{1,0:T(8,128)(2,1)S(1)} collective-permute-done((bf16[1280,128]{1,0:T(8,128)(2,1)S(1)}, bf16[1280,128]{1,0:T(8,128)(2,1)S(1)}, u32[]{:S(2)}, u32[]{:S(2)}) %collective-permute-start.9) | collective-permute-done | bytes 327712 | tf_op jit(solution)/shard_map/ppermute | solution.py:314
  35.0 3.4 %far.1 = (f32[128,5120]{1,0:T(8,128)S(1)}, f32[8,5120]{1,0:T(8,128)S(1)}) custom-call(s32[1]{0:T(128)S(4)} %get-tuple-element.28.first_ref, bf16[256,5120]{1,0:T(8,128)(2,1)S(1)} %get-tuple-element.29.qt_ref, bf16[640,128]{1,0:T(8,128)(2,1)S(1)} %collective-permute-done.6.f1, ...), custom_call_target="tpu_custom_call", output_to_operand_aliasing={{0}: (6, {}), {1}: (7, {})} | custom-call | flops 10066329600 | bytes 1048576 | tf_op jit(solution)/shard_map/far/pallas_call | solution.py:360
  38.4 6.3 %collective-permute-done.5.r2 = bf16[1280,128]{1,0:T(8,128)(2,1)S(1)} collective-permute-done((bf16[1280,128]{1,0:T(8,128)(2,1)S(1)}, bf16[1280,128]{1,0:T(8,128)(2,1)S(1)}, u32[]{:S(2)}, u32[]{:S(2)}) %collective-permute-start.5) | collective-permute-done | bytes 327712 | tf_op jit(solution)/shard_map/ppermute | solution.py:314
  44.7 0.8 %collective-permute-start.10 = (bf16[1280,128]{1,0:T(8,128)(2,1)S(1)}, bf16[1280,128]{1,0:T(8,128)(2,1)S(1)}, u32[]{:S(2)}, u32[]{:S(2)}) collective-permute-start(bf16[1280,128]{1,0:T(8,128)(2,1)S(1)} %collective-permute-done.5.r2), channel_id=1, source_target_pairs={{0,1},{1,0},{2,3},{3,2},{4,5},{5,4},{6,7},{7,6},{8,9},{9,8},{10,11... | collective-permute-start | bytes 983048 | tf_op jit(solution)/shard_map/ppermute | solution.py:314
  45.5 1.3 %collective-permute-done.10.t2 = bf16[1280,128]{1,0:T(8,128)(2,1)S(1)} collective-permute-done((bf16[1280,128]{1,0:T(8,128)(2,1)S(1)}, bf16[1280,128]{1,0:T(8,128)(2,1)S(1)}, u32[]{:S(2)}, u32[]{:S(2)}) %collective-permute-start.10) | collective-permute-done | bytes 327712 | tf_op jit(solution)/shard_map/ppermute | solution.py:314
  46.7 2.1 %last.1 = bf16[320,2048]{1,0:T(8,128)(2,1)} custom-call(s32[1]{0:T(128)S(4)} %get-tuple-element.28.first_ref, bf16[256,5120]{1,0:T(8,128)(2,1)S(1)} %get-tuple-element.29.qt_ref, bf16[1280,128]{1,0:T(8,128)(2,1)S(1)} %collective-permute-done.5.r2, bf16[1280,128]{1,0:T(8,128)(2,1)S(1)} %collective-permute-done.10.t2, ...), custom_call_target="tpu_custom_call" | custom-call | flops 6710886400 | bytes 1048576 | tf_op jit(solution)/shard_map/last/pallas_call | solution.py:374
  (5 shorter events, 0.1 us)
Async XLA Ops:
  1.0 11.0 %collective-permute-start = (bf16[640,128]{1,0:T(8,128)(2,1)S(1)}, bf16[640,128]{1,0:T(8,128)(2,1)S(1)}, u32[]{:S(2)}, u32[]{:S(2)}) collective-permute-start(bf16[640,128]{1,0:T(8,128)(2,1)S(1)} %pack.1.kv_ref.own), channel_id=1, source_target_pairs={{0,8},{1,9},{2,10},{3,11},{4,12},{5,13},{6,14},{7,15},{8,16},{9,17... | collective-permute-start | bytes 491528 | tf_op jit(solution)/shard_map/ppermute | solution.py:314
  12.0 3.8 %collective-permute-start.4 = (bf16[640,128]{1,0:T(8,128)(2,1)S(1)}, bf16[640,128]{1,0:T(8,128)(2,1)S(1)}, u32[]{:S(2)}, u32[]{:S(2)}) collective-permute-start(bf16[640,128]{1,0:T(8,128)(2,1)S(1)} %collective-permute-done.z), channel_id=1, source_target_pairs={{0,1},{1,0},{2,3},{3,2},{4,5},{5,4},{6,7},{7,6},{8,9},{9,8},{10,11... | collective-permute-start | bytes 491528 | tf_op jit(solution)/shard_map/ppermute | solution.py:314
  13.2 9.2 %collective-permute-start.3 = (bf16[640,128]{1,0:T(8,128)(2,1)S(1)}, bf16[640,128]{1,0:T(8,128)(2,1)S(1)}, u32[]{:S(2)}, u32[]{:S(2)}) collective-permute-start(bf16[640,128]{1,0:T(8,128)(2,1)S(1)} %collective-permute-done.z), channel_id=1, source_target_pairs={{0,8},{1,9},{2,10},{3,11},{4,12},{5,13},{6,14},{7,15},{8,16},{9,17... | collective-permute-start | bytes 491528 | tf_op jit(solution)/shard_map/ppermute | solution.py:314
  13.3 9.1 %collective-permute-start.2 = (bf16[640,128]{1,0:T(8,128)(2,1)S(1)}, bf16[640,128]{1,0:T(8,128)(2,1)S(1)}, u32[]{:S(2)}, u32[]{:S(2)}) collective-permute-start(bf16[640,128]{1,0:T(8,128)(2,1)S(1)} %get-tuple-element.55), channel_id=1, source_target_pairs={{0,6},{1,7},{2,0},{3,1},{4,2},{5,3},{6,4},{7,5},{8,14},{9,15},{10,... | collective-permute-start | bytes 491528 | tf_op jit(solution)/shard_map/ppermute | solution.py:314
  15.8 6.7 %collective-permute-start.1 = (bf16[640,128]{1,0:T(8,128)(2,1)S(1)}, bf16[640,128]{1,0:T(8,128)(2,1)S(1)}, u32[]{:S(2)}, u32[]{:S(2)}) collective-permute-start(bf16[640,128]{1,0:T(8,128)(2,1)S(1)} %get-tuple-element.56), channel_id=1, source_target_pairs={{0,2},{1,3},{2,4},{3,5},{4,6},{5,7},{6,0},{7,1},{8,10},{9,11},{10,... | collective-permute-start | bytes 491528 | tf_op jit(solution)/shard_map/ppermute | solution.py:314
  22.6 3.2 %collective-permute-start.8 = (bf16[1920,128]{1,0:T(8,128)(2,1)S(1)}, bf16[1920,128]{1,0:T(8,128)(2,1)S(1)}, u32[]{:S(2)}, u32[]{:S(2)}) collective-permute-start(bf16[1920,128]{1,0:T(8,128)(2,1)S(1)} %pad_maximum_fusion), channel_id=1, source_target_pairs={{0,1},{1,0},{2,3},{3,2},{4,5},{5,4},{6,7},{7,6},{8,9},{9,8},{10,11... | collective-permute-start | bytes 1474568 | tf_op jit(solution)/shard_map/ppermute | solution.py:314
  23.8 5.8 %collective-permute-start.7 = (bf16[640,128]{1,0:T(8,128)(2,1)S(1)}, bf16[640,128]{1,0:T(8,128)(2,1)S(1)}, u32[]{:S(2)}, u32[]{:S(2)}) collective-permute-start(bf16[640,128]{1,0:T(8,128)(2,1)S(1)} %get-tuple-element.51), channel_id=1, source_target_pairs={{0,6},{1,7},{2,0},{3,1},{4,2},{5,3},{6,4},{7,5},{8,14},{9,15},{10,... | collective-permute-start | bytes 491528 | tf_op jit(solution)/shard_map/ppermute | solution.py:314
  25.8 6.6 %collective-permute-start.6 = (bf16[640,128]{1,0:T(8,128)(2,1)S(1)}, bf16[640,128]{1,0:T(8,128)(2,1)S(1)}, u32[]{:S(2)}, u32[]{:S(2)}) collective-permute-start(bf16[640,128]{1,0:T(8,128)(2,1)S(1)} %get-tuple-element.52), channel_id=1, source_target_pairs={{0,2},{1,3},{2,4},{3,5},{4,6},{5,7},{6,0},{7,1},{8,10},{9,11},{10,... | collective-permute-start | bytes 491528 | tf_op jit(solution)/shard_map/ppermute | solution.py:314
  32.5 2.5 %collective-permute-start.9 = (bf16[1280,128]{1,0:T(8,128)(2,1)S(1)}, bf16[1280,128]{1,0:T(8,128)(2,1)S(1)}, u32[]{:S(2)}, u32[]{:S(2)}) collective-permute-start(bf16[1280,128]{1,0:T(8,128)(2,1)S(1)} %pad_maximum_fusion.2), channel_id=1, source_target_pairs={{0,1},{1,0},{2,3},{3,2},{4,5},{5,4},{6,7},{7,6},{8,9},{9,8},{10,11... | collective-permute-start | bytes 983048 | tf_op jit(solution)/shard_map/ppermute | solution.py:314
  33.8 10.9 %collective-permute-start.5 = (bf16[1280,128]{1,0:T(8,128)(2,1)S(1)}, bf16[1280,128]{1,0:T(8,128)(2,1)S(1)}, u32[]{:S(2)}, u32[]{:S(2)}) collective-permute-start(bf16[1280,128]{1,0:T(8,128)(2,1)S(1)} %pad_maximum_fusion.1), channel_id=1, source_target_pairs={{0,4},{1,5},{2,6},{3,7},{4,0},{5,1},{6,2},{7,3},{8,12},{9,13},{10,... | collective-permute-start | bytes 983048 | tf_op jit(solution)/shard_map/ppermute | solution.py:314
  44.7 2.1 %collective-permute-start.10 = (bf16[1280,128]{1,0:T(8,128)(2,1)S(1)}, bf16[1280,128]{1,0:T(8,128)(2,1)S(1)}, u32[]{:S(2)}, u32[]{:S(2)}) collective-permute-start(bf16[1280,128]{1,0:T(8,128)(2,1)S(1)} %collective-permute-done.5.r2), channel_id=1, source_target_pairs={{0,1},{1,0},{2,3},{3,2},{4,5},{5,4},{6,7},{7,6},{8,9},{9,8},{10,11... | collective-permute-start | bytes 983048 | tf_op jit(solution)/shard_map/ppermute | solution.py:314
